TPU v7x, 32 devices: a whole 2x2x4 slice. The times are simulated.
32 devices in a mesh: groups: 2 (over y), fsdp: 8 (over z, x), dp: 1, sub: 2 (over core).
Axes of the slice: x: 2, y: 2, z: 4, core: 2. Of those that a mesh axis runs over, the one named last changes fastest.
Arguments:
- features: bfloat16 [16, 768, 1280], P(('groups', 'fsdp', 'dp'), 'sub'), parts along dimension 0, may hold values from -6 to 6
- golden: bfloat16 [4, 768, 1280], P(('groups', 'dp'), 'sub'), parts along dimension 0, may hold values from -6 to 6
- die_wafer: int32 [16], P(('groups', 'fsdp', 'dp')), parts along dimension 0, may hold values from 0 to 1
- norm_gain: float32 [1280], replicated, may hold values from 0.1 to 1.9
- proj_weight: bfloat16 [1280, 2560], P('fsdp'), may hold values from -0.15625 to 0.15625
- out_weight: bfloat16 [2560, 1280], P('fsdp'), may hold values from -0.125 to 0.125
- zero_weight: bfloat16 [1280, 1280], P(None, 'fsdp'), may hold values from -0.15625 to 0.15625
Outputs:
- block_out: bfloat16 [16, 768, 1280], P(('groups', 'fsdp', 'dp'), 'sub'), parts along dimension 0
There are 2 independent parts, one for each index of `groups`. A program takes and returns all parts, laid end to end along the dimension named above; an argument that names none is the same for every part. Nothing has to cross between parts.
All inputs are finite; a program needn't handle non-finite values.
Results may differ from a plain program's by a relative error of at most 0.005.
Values may be sent and summed in bfloat16 or wider, within the bound.
A program may use at most 128 MiB of HBM per device.

v0:
```python
import jax
import jax.numpy as jnp
from jax import lax
from jax.sharding import PartitionSpec as P


def body(features, golden, die_wafer, norm_gain, proj_weight, out_weight, zero_weight):
    wafer_one = die_wafer[0]
    columns = jnp.einsum(
        "wpc,cd->wpd", golden, zero_weight, preferred_element_type=jnp.float32
    ).astype(jnp.bfloat16)
    gathered = lax.all_gather(columns, "fsdp", axis=2, tiled=True)
    residual = lax.dynamic_index_in_dim(gathered, wafer_one, 0, keepdims=False)
    mixed = features[0].astype(jnp.float32) + residual.astype(jnp.float32)
    average = jnp.mean(mixed, axis=-1, keepdims=True)
    centred = mixed - average
    variance = jnp.mean(centred * centred, axis=-1, keepdims=True)
    normed = (centred * lax.rsqrt(variance + 1e-05) * norm_gain).astype(jnp.bfloat16)
    inputs = normed
    preact = jnp.dot(
        inputs,
        lax.all_gather(proj_weight, "fsdp", axis=0, tiled=True),
        preferred_element_type=jnp.float32,
    )
    hidden = jax.nn.gelu(preact, approximate=True).astype(jnp.bfloat16)
    inputs = hidden
    branch = jnp.dot(
        inputs,
        lax.all_gather(out_weight, "fsdp", axis=0, tiled=True),
        preferred_element_type=jnp.float32,
    )
    return (mixed + branch).astype(jnp.bfloat16)[None]


def solution(mesh):
    placed = (
        P(("groups", "fsdp", "dp"), "sub", None),
        P(("groups", "dp"), "sub", None),
        P(("groups", "fsdp", "dp")),
        P(),
        P("fsdp", None),
        P("fsdp", None),
        P(None, "fsdp"),
    )
    return jax.shard_map(
        body,
        mesh=mesh,
        in_specs=placed,
        out_specs=P(("groups", "fsdp", "dp"), "sub", None),
        check_vma=False,
    )
```

profile of v0, /device:TPU:0, one launch (start us, length us, event | category | flops | bytes accessed | tf_op | source)
XLA Modules:
  0.0 289.0 jit_solution(17761163579044327469)
XLA Ops:
  6.5 0.0 copy-start
  6.5 0.0 all-gather.4.cloned.1.call-start
  6.5 1.5 copy-done
  8.1 2.5 convolution_convert_fusion
  10.6 0.0 all-gather.4.cloned.1.call-update
  10.6 0.0 all-gather.6.cloned.1.call-start
  10.7 0.7 all-gather.6.cloned.1.call-update
  11.4 0.0 all-gather.8.cloned.1.call-start
  11.4 0.7 all-gather.8.cloned.1.call-update
  12.7 1.6 copy.8
  14.3 46.6 %all-gather.4.cloned.1.call-done = bf16[2,384,1280]{1,2,0:T(8,128)(2,1)} async-done(((bf16[2,384,160]{1,2,0:T(8,128)(2,1)}), bf16[2,384,1280]{1,2,0:T(8,128)(2,1)}) %all-gather.4.cloned.1.call-update) | async-done | bytes 1966096 | tf_op jit(solution)/shard_map/all_gather | solution.py:12
  61.0 0.0 copy-start.1
  61.0 0.0 copy-start.2
  61.0 1.7 fusion.15
  62.7 0.1 copy-done.1
  62.8 0.4 multiply_reduce_fusion
  63.3 101.3 %all-gather.6.cloned.1.call-done = bf16[1280,2560]{1,0:T(8,128)(2,1)} async-done(((bf16[160,2560]{1,0:T(8,128)(2,1)}), bf16[1280,2560]{1,0:T(8,128)(2,1)}) %all-gather.6.cloned.1.call-update) | async-done | bytes 6553616 | tf_op jit(solution)/shard_map/all_gather | solution.py:22
  164.5 102.6 %all-gather.8.cloned.1.call-done = bf16[2560,1280]{1,0:T(8,128)(2,1)} async-done(((bf16[320,1280]{1,0:T(8,128)(2,1)}), bf16[2560,1280]{1,0:T(8,128)(2,1)}) %all-gather.8.cloned.1.call-update) | async-done | bytes 6553616 | tf_op jit(solution)/shard_map/all_gather | solution.py:29
  267.2 0.0 copy-done.2
  267.2 13.0 %fusion.9 = bf16[1,384,1280]{1,2,0:T(8,128)(2,1)} fusion(bf16[2560,1280]{1,0:T(8,128)(2,1)} %all-gather.8.cloned.1.call-done, bf16[1,384,1280]{1,2,0:T(8,128)(2,1)S(1)} %copy.8, bf16[1280,2560]{1,0:T(8,128)(2,1)} %all-gather.6.cloned.1.call-done, f32[1280]{0:T(1024)S(1)} %copy-done.2, f32[384]{0:T(512)S(1)} %add_rsqrt_fusion, ...), kind=kOutput, calls=%fused_computation.11 | convolution fusion | flops 5047910400 | bytes 18035712 | tf_op jit(solution)/shard_map/dot_general | solution.py:27
  280.2 2.2 copy.10
  (2 shorter events, 0.0 us)
Async XLA Ops:
  6.5 1.5 copy-start
  6.5 54.4 %all-gather.4.cloned.1.call-start = ((), (), s32[]{:S(2)}) async-start(), calls=%async_computation | async-start | bytes 2211840 | tf_op jit(solution)/shard_map/all_gather | solution.py:12
  10.6 153.9 %all-gather.6.cloned.1.call-start = ((), (), s32[]{:S(2)}) async-start(), calls=%async_computation.1 | async-start | bytes 7372800 | tf_op jit(solution)/shard_map/all_gather | solution.py:22
  11.4 255.8 %all-gather.8.cloned.1.call-start = ((), (), s32[]{:S(2)}) async-start(), calls=%async_computation.2 | async-start | bytes 7372800 | tf_op jit(solution)/shard_map/all_gather | solution.py:29
  61.0 1.8 copy-start.1
  61.0 206.2 %copy-start.2 = (f32[1280]{0:T(1024)S(1)}, f32[1280]{0:T(1024)}, u32[]{:S(2)}) copy-start(f32[1280]{0:T(1024)} %param.10) | copy-start | bytes 15364
Sparse Core Ops, SparseCore 0:
  10.7 50.2 all-gather.3
  63.2 101.3 all-gather.5
  166.7 100.3 all-gather.7
where the time goes:
time: 289 us
  waiting for transfers between devices  252 us (87%)
  matrix products  15.5 us (5%)
  between operations  13.8 us (5%)
  local copies, waits for them, and re-layouts  5.51 us (2%)
    all_gather x1, waiting for transfers between devices, body(): lax.all_gather(out_weight, 'fsdp', axis=0, tiled=True)  103 us
    all_gather x1, waiting for transfers between devices, body(): lax.all_gather(proj_weight, 'fsdp', axis=0, tiled=True)  101 us
    all_gather x1, waiting for transfers between devices, body(): gathered = lax.all_gather(columns, 'fsdp', axis=2, tiled=True)  46.6 us
    dot_general x1, matrix products, body(): jnp.dot(inputs, lax.all_gather(out_weight, 'fsdp', axis=0, tiled=True), p...  13 us
  transfers between devices with their start and end apart: 3, of which 3 were waited for; matrix products, arithmetic and copies ran while one was open for 1% of the time, Pallas kernels for 0%

commit v1 on v0

--- a/solution.py
+++ b/solution.py
@@ -2,6 +2,12 @@
 import jax.numpy as jnp
 from jax import lax
 from jax.sharding import PartitionSpec as P
+
+
+def in_order(tiles, dim):
+    shape = list(tiles.shape[1:])
+    shape[dim] *= tiles.shape[0]
+    return jnp.moveaxis(tiles, 0, dim).reshape(shape)
 
 
 def body(features, golden, die_wafer, norm_gain, proj_weight, out_weight, zero_weight):
@@ -9,7 +15,19 @@
     columns = jnp.einsum(
         "wpc,cd->wpd", golden, zero_weight, preferred_element_type=jnp.float32
     ).astype(jnp.bfloat16)
-    gathered = lax.all_gather(columns, "fsdp", axis=2, tiled=True)
+    size = lax.axis_size("fsdp")
+    pairs = [(i, (i + 1) % size) for i in range(size)]
+    back = [(b, a) for a, b in pairs]
+    lower, upper = ([], [])
+    for step in range(size - 1):
+        if step % 2 == 0:
+            lower.append(lax.ppermute(lower[-1] if lower else columns, "fsdp", pairs))
+        else:
+            upper.append(lax.ppermute(upper[-1] if upper else columns, "fsdp", back))
+    blocks = jnp.stack([*lower[::-1], columns, *upper])
+    shift = lax.axis_index("fsdp") - len(lower)
+    blocks = blocks[(jnp.arange(size) - shift) % size]
+    gathered = in_order(blocks, 2)
     residual = lax.dynamic_index_in_dim(gathered, wafer_one, 0, keepdims=False)
     mixed = features[0].astype(jnp.float32) + residual.astype(jnp.float32)
     average = jnp.mean(mixed, axis=-1, keepdims=True)

time: 289 us -> 252 us (0.87)
  waiting for transfers between devices: 252 us -> 190 us
  starting transfers between devices: 0.08 us -> 16.6 us
  local copies, waits for them, and re-layouts: 5.51 us -> 14.8 us
    all_gather x1, waiting for transfers between devices: 101 us -> 44.8 us  [body(): lax.all_gather(proj_weight, 'fsdp', axis=0, tiled=True)]
    all_gather x1 -> x0, waiting for transfers between devices: 46.6 us -> none  [body(): gathered = lax.all_gather(columns, 'fsdp', axis=2, tiled=True)]
    ppermute x0 -> x7, waiting for transfers between devices: none -> 41.6 us  [the longest x4 41 us: body(): lower.append(lax.ppermute(lower[-1] if lower else columns, 'fsdp', pairs))]
    ppermute x0 -> x7, starting transfers between devices: none -> 16.6 us  [the longest x3 11.7 us: body(): upper.append(lax.ppermute(upper[-1] if upper else columns, 'fsdp', back))]
    unnamed x7 -> x14, local copies, waits for them, and re-layouts: 3.28 us -> 7.64 us
    gather x0 -> x1, local copies, waits for them, and re-layouts: none -> 3.64 us  [body(): blocks = blocks[(jnp.arange(size) - shift) % size]]
  transfers between devices with their start and end apart: 3 -> 9, of which waited for: 3 -> 7; matrix products, arithmetic and copies ran while one was open for 1% -> 7% of each run, Pallas kernels for 0% -> 0%
where the time goes in v1:
time: 252 us
  waiting for transfers between devices  190 us (75%)
  starting transfers between devices  16.6 us (7%)
  local copies, waits for them, and re-layouts  14.8 us (6%)
  between operations  14.1 us (6%)
  matrix products  13.5 us (5%)
    all_gather x1, waiting for transfers between devices, body(): lax.all_gather(out_weight, 'fsdp', axis=0, tiled=True)  103 us
    all_gather x1, waiting for transfers between devices, body(): lax.all_gather(proj_weight, 'fsdp', axis=0, tiled=True)  44.8 us
    ppermute x4, waiting for transfers between devices, body(): lower.append(lax.ppermute(lower[-1] if lower else columns, 'fsdp', pairs))  41 us
    ppermute x3, starting transfers between devices, body(): upper.append(lax.ppermute(upper[-1] if upper else columns, 'fsdp', back))  11.7 us
    dot_general x1, matrix products, body(): jnp.dot(inputs, lax.all_gather(out_weight, 'fsdp', axis=0, tiled=True), p...  11.7 us
    unnamed x14, local copies, waits for them, and re-layouts  7.64 us
  transfers between devices with their start and end apart: 9, of which 7 were waited for; matrix products, arithmetic and copies ran while one was open for 7% of the time, Pallas kernels for 0%

profile of v1, /device:TPU:0, one launch (start us, length us, event | category | flops | bytes accessed | tf_op | source)
XLA Modules:
  0.0 251.6 jit_solution(8641852326645881122)
XLA Ops:
  8.1 1.8 convolution_convert_fusion
  9.9 3.0 %collective-permute-start = (bf16[2,384,160]{1,2,0:T(8,128)(2,1)S(1)}, bf16[2,384,160]{1,2,0:T(8,128)(2,1)S(1)}, u32[]{:S(2)}, u32[]{:S(2)}) collective-permute-start(bf16[2,384,160]{1,2,0:T(8,128)(2,1)S(1)} %convolution_convert_fusion), channel_id=1, source_target_pairs={{0,2},{2,4},{4,6},{6,8},{8,10},{10,12},{12,14},{14,0},{1,3},{3,5},... | collective-permute-start | bytes 737288 | tf_op jit(solution)/shard_map/ppermute | solution.py:24
  12.9 9.0 %collective-permute-done = bf16[2,384,160]{1,2,0:T(8,128)(2,1)S(1)} collective-permute-done((bf16[2,384,160]{1,2,0:T(8,128)(2,1)S(1)}, bf16[2,384,160]{1,2,0:T(8,128)(2,1)S(1)}, u32[]{:S(2)}, u32[]{:S(2)}) %collective-permute-start) | collective-permute-done | bytes 245792 | tf_op jit(solution)/shard_map/ppermute | solution.py:24
  21.9 4.7 %collective-permute-start.4 = (bf16[2,384,160]{1,2,0:T(8,128)(2,1)S(1)}, bf16[2,384,160]{1,2,0:T(8,128)(2,1)S(1)}, u32[]{:S(2)}, u32[]{:S(2)}) collective-permute-start(bf16[2,384,160]{1,2,0:T(8,128)(2,1)S(1)} %convolution_convert_fusion), channel_id=1, source_target_pairs={{2,0},{4,2},{6,4},{8,6},{10,8},{12,10},{14,12},{0,14},{3,1},{5,3},... | collective-permute-start | bytes 737288 | tf_op jit(solution)/shard_map/ppermute | solution.py:26
  26.6 11.4 %collective-permute-done.1 = bf16[2,384,160]{1,2,0:T(8,128)(2,1)S(1)} collective-permute-done((bf16[2,384,160]{1,2,0:T(8,128)(2,1)S(1)}, bf16[2,384,160]{1,2,0:T(8,128)(2,1)S(1)}, u32[]{:S(2)}, u32[]{:S(2)}) %collective-permute-start.1) | collective-permute-done | bytes 245792 | tf_op jit(solution)/shard_map/ppermute | solution.py:24
  38.0 1.9 collective-permute-start.2
  40.5 2.2 collective-permute-start.5
  42.8 11.3 %collective-permute-done.2 = bf16[2,384,160]{1,2,0:T(8,128)(2,1)S(1)} collective-permute-done((bf16[2,384,160]{1,2,0:T(8,128)(2,1)S(1)}, bf16[2,384,160]{1,2,0:T(8,128)(2,1)S(1)}, u32[]{:S(2)}, u32[]{:S(2)}) %collective-permute-start.2) | collective-permute-done | bytes 245792 | tf_op jit(solution)/shard_map/ppermute | solution.py:24
  54.7 4.8 %collective-permute-start.6 = (bf16[2,384,160]{1,2,0:T(8,128)(2,1)S(1)}, bf16[2,384,160]{1,2,0:T(8,128)(2,1)S(1)}, u32[]{:S(2)}, u32[]{:S(2)}) collective-permute-start(bf16[2,384,160]{1,2,0:T(8,128)(2,1)S(1)} %collective-permute-done.5), channel_id=1, source_target_pairs={{2,0},{4,2},{6,4},{8,6},{10,8},{12,10},{14,12},{0,14},{3,1},{5,3},... | collective-permute-start | bytes 737288 | tf_op jit(solution)/shard_map/ppermute | solution.py:26
  59.5 9.3 %collective-permute-done.3 = bf16[2,384,160]{1,2,0:T(8,128)(2,1)} collective-permute-done((bf16[2,384,160]{1,2,0:T(8,128)(2,1)S(1)}, bf16[2,384,160]{1,2,0:T(8,128)(2,1)}, u32[]{:S(2)}, u32[]{:S(2)}) %collective-permute-start.3) | collective-permute-done | bytes 245792 | tf_op jit(solution)/shard_map/ppermute | solution.py:24
  68.8 1.7 bitcast_dynamic-update-slice_fusion.7
  70.5 0.7 bitcast_dynamic-update-slice_fusion.6
  71.2 0.7 bitcast_dynamic-update-slice_fusion.5
  71.9 0.7 bitcast_dynamic-update-slice_fusion.4
  74.1 0.7 bitcast_dynamic-update-slice_fusion.1
  74.8 0.7 bitcast_dynamic-update-slice_fusion
  75.5 3.6 %gather_fusion = bf16[8,2,384,160]{2,3,1,0:T(8,128)(2,1)} fusion(bf16[8,2,384,160]{2,3,1,0:T(8,128)(2,1)} %bitcast_dynamic-update-slice_fusion, s32[1024]{0:T(1024)S(1)} %pad_clamp_fusion), kind=kCustom, calls=%fused_computation | custom fusion | bytes 3932192 | tf_op jit(solution)/shard_map/gather | solution.py:29
  79.2 1.7 copy.8
  80.9 1.1 constant_dynamic-slice_fusion
  82.0 1.5 copy.10
  83.6 1.6 fusion.15
  85.7 44.8 %all-gather.3.cloned.1.call-done = bf16[1280,2560]{1,0:T(8,128)(2,1)} async-done(((bf16[160,2560]{1,0:T(8,128)(2,1)}), bf16[1280,2560]{1,0:T(8,128)(2,1)}) %all-gather.3.cloned.1.call-update) | async-done | bytes 6553616 | tf_op jit(solution)/shard_map/all_gather | solution.py:40
  130.5 102.6 %all-gather.5.cloned.1.call-done = bf16[2560,1280]{1,0:T(8,128)(2,1)} async-done(((bf16[320,1280]{1,0:T(8,128)(2,1)}), bf16[2560,1280]{1,0:T(8,128)(2,1)}) %all-gather.5.cloned.1.call-update) | async-done | bytes 6553616 | tf_op jit(solution)/shard_map/all_gather | solution.py:47
  233.1 11.7 %fusion.9 = bf16[1,384,1280]{2,1,0:T(8,128)(2,1)} fusion(bf16[2560,1280]{1,0:T(8,128)(2,1)} %all-gather.5.cloned.1.call-done, bf16[1,384,1280]{2,1,0:T(8,128)(2,1)S(1)} %copy.10, bf16[1,384,1280]{2,1,0:T(8,128)(2,1)} %param.7, bf16[1280,2560]{1,0:T(8,128)(2,1)} %all-gather.3.cloned.1.call-done, f32[1280]{0:T(1024)S(1)} %copy-done.2, ...), kind=kOutput, calls=%fused_computation.12 | convolution fusion | flops 5047910400 | bytes 16064512 | tf_op jit(solution)/shard_map/dot_general | solution.py:45
  (22 shorter events, 4.1 us)
Async XLA Ops:
  6.5 1.5 copy-start
  6.5 123.9 %all-gather.3.cloned.1.call-start = ((), (), s32[]{:S(2)}) async-start(), calls=%async_computation | async-start | bytes 7372800 | tf_op jit(solution)/shard_map/all_gather | solution.py:40
  7.3 225.8 %all-gather.5.cloned.1.call-start = ((), (), s32[]{:S(2)}) async-start(), calls=%async_computation.1 | async-start | bytes 7372800 | tf_op jit(solution)/shard_map/all_gather | solution.py:47
  9.9 12.0 %collective-permute-start = (bf16[2,384,160]{1,2,0:T(8,128)(2,1)S(1)}, bf16[2,384,160]{1,2,0:T(8,128)(2,1)S(1)}, u32[]{:S(2)}, u32[]{:S(2)}) collective-permute-start(bf16[2,384,160]{1,2,0:T(8,128)(2,1)S(1)} %convolution_convert_fusion), channel_id=1, source_target_pairs={{0,2},{2,4},{4,6},{6,8},{8,10},{10,12},{12,14},{14,0},{1,3},{3,5},... | collective-permute-start | bytes 737288 | tf_op jit(solution)/shard_map/ppermute | solution.py:24
  21.9 16.2 %collective-permute-start.1 = (bf16[2,384,160]{1,2,0:T(8,128)(2,1)S(1)}, bf16[2,384,160]{1,2,0:T(8,128)(2,1)S(1)}, u32[]{:S(2)}, u32[]{:S(2)}) collective-permute-start(bf16[2,384,160]{1,2,0:T(8,128)(2,1)S(1)} %collective-permute-done), channel_id=1, source_target_pairs={{0,2},{2,4},{4,6},{6,8},{8,10},{10,12},{12,14},{14,0},{1,3},{3,5},... | collective-permute-start | bytes 737288 | tf_op jit(solution)/shard_map/ppermute | solution.py:24
  21.9 18.7 %collective-permute-start.4 = (bf16[2,384,160]{1,2,0:T(8,128)(2,1)S(1)}, bf16[2,384,160]{1,2,0:T(8,128)(2,1)S(1)}, u32[]{:S(2)}, u32[]{:S(2)}) collective-permute-start(bf16[2,384,160]{1,2,0:T(8,128)(2,1)S(1)} %convolution_convert_fusion), channel_id=1, source_target_pairs={{2,0},{4,2},{6,4},{8,6},{10,8},{12,10},{14,12},{0,14},{3,1},{5,3},... | collective-permute-start | bytes 737288 | tf_op jit(solution)/shard_map/ppermute | solution.py:26
  38.0 16.0 %collective-permute-start.2 = (bf16[2,384,160]{1,2,0:T(8,128)(2,1)S(1)}, bf16[2,384,160]{1,2,0:T(8,128)(2,1)S(1)}, u32[]{:S(2)}, u32[]{:S(2)}) collective-permute-start(bf16[2,384,160]{1,2,0:T(8,128)(2,1)S(1)} %collective-permute-done.1), channel_id=1, source_target_pairs={{0,2},{2,4},{4,6},{6,8},{8,10},{10,12},{12,14},{14,0},{1,3},{3,5},... | collective-permute-start | bytes 737288 | tf_op jit(solution)/shard_map/ppermute | solution.py:24
  40.5 14.2 %collective-permute-start.5 = (bf16[2,384,160]{1,2,0:T(8,128)(2,1)S(1)}, bf16[2,384,160]{1,2,0:T(8,128)(2,1)S(1)}, u32[]{:S(2)}, u32[]{:S(2)}) collective-permute-start(bf16[2,384,160]{1,2,0:T(8,128)(2,1)S(1)} %collective-permute-done.4), channel_id=1, source_target_pairs={{2,0},{4,2},{6,4},{8,6},{10,8},{12,10},{14,12},{0,14},{3,1},{5,3},... | collective-permute-start | bytes 737288 | tf_op jit(solution)/shard_map/ppermute | solution.py:26
  54.0 14.8 %collective-permute-start.3 = (bf16[2,384,160]{1,2,0:T(8,128)(2,1)S(1)}, bf16[2,384,160]{1,2,0:T(8,128)(2,1)}, u32[]{:S(2)}, u32[]{:S(2)}) collective-permute-start(bf16[2,384,160]{1,2,0:T(8,128)(2,1)S(1)} %collective-permute-done.2), channel_id=1, source_target_pairs={{0,2},{2,4},{4,6},{6,8},{8,10},{10,12},{12,14},{14,0},{1,3},{3,5},... | collective-permute-start | bytes 737288 | tf_op jit(solution)/shard_map/ppermute | solution.py:24
  54.7 20.1 %collective-permute-start.6 = (bf16[2,384,160]{1,2,0:T(8,128)(2,1)S(1)}, bf16[2,384,160]{1,2,0:T(8,128)(2,1)S(1)}, u32[]{:S(2)}, u32[]{:S(2)}) collective-permute-start(bf16[2,384,160]{1,2,0:T(8,128)(2,1)S(1)} %collective-permute-done.5), channel_id=1, source_target_pairs={{2,0},{4,2},{6,4},{8,6},{10,8},{12,10},{14,12},{0,14},{3,1},{5,3},... | collective-permute-start | bytes 737288 | tf_op jit(solution)/shard_map/ppermute | solution.py:26
  83.5 1.7 copy-start.1
  83.6 149.5 %copy-start.2 = (f32[1280]{0:T(1024)S(1)}, f32[1280]{0:T(1024)}, u32[]{:S(2)}) copy-start(f32[1280]{0:T(1024)} %param.10) | copy-start | bytes 15364
Sparse Core Ops, SparseCore 0:
  9.5 120.8 all-gather.2
  132.6 100.3 all-gather.4
